TPU v7x, 32 devices: a whole 2x2x4 slice. The times are simulated.
32 devices in a mesh: dp: 2 (over y), mp: 16 (over z, x, core).
Axes of the slice: x: 2, y: 2, z: 4, core: 2. Of those that a mesh axis runs over, the one named last changes fastest.
Arguments:
- tokens: bfloat16 [4096, 2, 768], P('mp', 'dp'), may hold values from -6 to 6
- cotangent: bfloat16 [4096, 2, 768], P('mp', 'dp'), may hold values from -6 to 6
- weight_in: float32 [2, 768, 3072], P(None, None, 'mp'), may hold values from -0.21650635 to 0.21650635
- bias_in: float32 [2, 3072], P(None, 'mp'), may hold values from -1.2 to 1.2
- weight_out: float32 [2, 3072, 768], P(None, 'mp'), may hold values from -0.108253175 to 0.108253175
- vectors: float32 [2, 5, 768], replicated, may hold values from -1 to 2
- moment_in: float32 [2, 768, 3072], P(None, None, 'mp'), may hold values from -0.0029296875 to 0.0029296875
- square_in: float32 [2, 768, 3072], P(None, None, 'mp'), may hold values from 2.5431316e-08 to 1.695421e-07
- moment_bias: float32 [2, 3072], P(None, 'mp'), may hold values from -0.0029296875 to 0.0029296875
- square_bias: float32 [2, 3072], P(None, 'mp'), may hold values from 2.5431316e-08 to 1.695421e-07
- moment_out: float32 [2, 3072, 768], P(None, 'mp'), may hold values from -0.005859375 to 0.005859375
- square_out: float32 [2, 3072, 768], P(None, 'mp'), may hold values from 1.05963814e-07 to 6.781684e-07
- moment_vec: float32 [2, 5, 768], replicated, may hold values from -0.009765625 to 0.009765625
- square_vec: float32 [2, 5, 768], replicated, may hold values from 2.966987e-07 to 1.695421e-06
Outputs:
- activations: bfloat16 [4096, 2, 768], P('mp', 'dp')
- input_grad: float32 [4096, 2, 768], P('mp', 'dp')
- grad_norm: float32 [], replicated
- new_moment_in: float32 [2, 768, 3072], P(None, None, 'mp')
- new_square_in: float32 [2, 768, 3072], P(None, None, 'mp')
- new_weight_in: float32 [2, 768, 3072], P(None, None, 'mp')
- copy_in: bfloat16 [2, 768, 3072], P(None, None, 'mp')
- new_moment_out: float32 [2, 3072, 768], P(None, 'mp')
- new_square_out: float32 [2, 3072, 768], P(None, 'mp')
- new_weight_out: float32 [2, 3072, 768], P(None, 'mp')
- copy_out: bfloat16 [2, 3072, 768], P(None, 'mp')
- new_moment_bias: float32 [2, 3072], P(None, 'mp')
- new_square_bias: float32 [2, 3072], P(None, 'mp')
- new_bias_in: float32 [2, 3072], P(None, 'mp')
- new_moment_vec: float32 [2, 5, 768], replicated
- new_square_vec: float32 [2, 5, 768], replicated
- new_vectors: float32 [2, 5, 768], replicated
All inputs are finite; a program needn't handle non-finite values.
Results may differ from a plain program's by a relative error of at most 0.018.
Values may be sent and summed in bfloat16 or wider, within the bound.
A program may use at most 192 MiB of HBM per device.

v0:
```python
import math

import jax
import jax.numpy as jnp
from jax import lax
from jax.sharding import PartitionSpec as P

D = 768
FF = 3072
L = 4096
LAYERS = 2
STEP = 5


CLIP = 1.0
BETA_ONE = 0.5
BETA_TWO = 0.5
EPS_ADAM = 1e-08
EPS_NORM = 1e-05
DECAY = 0.01


def angles(row_ids, col_ids, period):
    product = row_ids[:, None] * col_ids[None, :] % period
    angle_grid = product.astype(jnp.float32) * (2.0 * math.pi / period)
    return (jnp.cos(angle_grid).astype(jnp.bfloat16), jnp.sin(angle_grid).astype(jnp.bfloat16))


def matmul(left_op, right_op):
    return jnp.dot(left_op, right_op, preferred_element_type=jnp.float32)


def inner_rows(left_op, right_op):
    return lax.dot_general(
        left_op, right_op, (((0,), (0,)), ((), ())), preferred_element_type=jnp.float32
    )


def inner_cols(left_op, right_op):
    return lax.dot_general(
        left_op, right_op, (((1,), (1,)), ((), ())), preferred_element_type=jnp.float32
    )


def layer_norm(value, gain, shift):
    centre = value - jnp.mean(value, axis=-1, keepdims=True)
    spread = jnp.mean(centre * centre, axis=-1, keepdims=True)
    return centre * lax.rsqrt(spread + EPS_NORM) * gain + shift


def adamw(weight, grad, moment, square, rate, decay):
    new_moment = BETA_ONE * moment + (1.0 - BETA_ONE) * grad
    new_square = BETA_TWO * square + (1.0 - BETA_TWO) * grad * grad
    moment_hat = new_moment / (1.0 - BETA_ONE**STEP)
    square_hat = new_square / (1.0 - BETA_TWO**STEP)
    new_weight = weight - rate * (moment_hat / (jnp.sqrt(square_hat) + EPS_ADAM) + decay * weight)
    return (new_moment, new_square, new_weight)


def on_device(
    tokens,
    cotangent,
    weight_in,
    bias_in,
    weight_out,
    vectors,
    moment_in,
    square_in,
    moment_bias,
    square_bias,
    moment_out,
    square_out,
    moment_vec,
    square_vec,
):
    row_count, seq_count, feat_count = tokens.shape
    offset = lax.axis_index("mp") * row_count
    own_rows = offset + jnp.arange(row_count, dtype=jnp.int32)
    feature_ids = jnp.arange(feat_count, dtype=jnp.int32)
    cos_feat, sin_feat = angles(feature_ids, feature_ids, feat_count)
    factor_mix = 1.0 / math.sqrt(L * D)
    current = tokens.astype(jnp.float32)
    saved = []
    for layer_at in range(LAYERS):
        vector_set = vectors[layer_at]
        rounded = current.astype(jnp.bfloat16)
        piece = lax.all_gather(rounded, "mp", axis=0, tiled=True)
        count = piece.shape[0]
        cosine, sine = angles(own_rows, jnp.arange(count, dtype=jnp.int32), L)
        flat = piece.reshape(count, -1)
        spec_cos = matmul(cosine, flat)
        spec_sin = matmul(sine, flat)
        spec_cos = spec_cos.astype(jnp.bfloat16)
        spec_sin = spec_sin.astype(jnp.bfloat16)
        mixed = (factor_mix * (matmul(spec_cos, cos_feat) - matmul(spec_sin, sin_feat))).reshape(
            row_count, seq_count, feat_count
        )
        summed = current + mixed
        normed = layer_norm(summed, vector_set[0], vector_set[1])
        hidden_in = normed.astype(jnp.bfloat16)
        weight_one = weight_in[layer_at].astype(jnp.bfloat16)
        weight_two = weight_out[layer_at].astype(jnp.bfloat16)
        bias_one = bias_in[layer_at].astype(jnp.bfloat16)
        whole_one, whole_two, whole_bias = (
            lax.all_gather(weight_one, "mp", axis=1, tiled=True),
            lax.all_gather(weight_two, "mp", axis=0, tiled=True),
            lax.all_gather(bias_one, "mp", axis=0, tiled=True),
        )
        inputs = hidden_in.reshape(-1, feat_count)
        pre_act = matmul(inputs, whole_one) + whole_bias.astype(jnp.float32)
        acts = jax.nn.gelu(pre_act).astype(jnp.bfloat16)
        branch = matmul(acts, whole_two).reshape(row_count, seq_count, feat_count)
        held = (inputs, whole_one, whole_two)
        total = normed + branch + vector_set[2]
        current = layer_norm(total, vector_set[3], vector_set[4])
        saved.append((summed, total, pre_act, acts, held))
    activations = current.astype(jnp.bfloat16)
    grad = cotangent.astype(jnp.float32)
    layer_grads = [None] * LAYERS
    for layer_at in reversed(range(LAYERS)):
        vector_set = vectors[layer_at]
        summed, total, pre_act, acts, held = saved[layer_at]
        inputs, mat_one, mat_two = held
        _, pull_out = jax.vjp(layer_norm, total, vector_set[3], vector_set[4])
        grad_total, gain_two, shift_two = pull_out(grad)
        grad_branch = grad_total.astype(jnp.bfloat16)
        grad_bias_two = jnp.sum(grad_branch.astype(jnp.float32), axis=(0, 1))
        flat_grad = grad_branch.reshape(-1, feat_count)
        grad_act = inner_cols(flat_grad, mat_two)
        _, pull_gelu = jax.vjp(jax.nn.gelu, pre_act)
        grad_pre = pull_gelu(grad_act)[0].astype(jnp.bfloat16)
        full_one = inner_rows(inputs, grad_pre)
        full_two = inner_rows(acts, flat_grad)
        full_bias = jnp.sum(grad_pre.astype(jnp.float32), axis=0)
        grad_one, grad_two, grad_bias_one = (
            lax.psum_scatter(
                full_one.astype(jnp.bfloat16), "mp", scatter_dimension=1, tiled=True
            ).astype(jnp.float32),
            lax.psum_scatter(
                full_two.astype(jnp.bfloat16), "mp", scatter_dimension=0, tiled=True
            ).astype(jnp.float32),
            lax.psum_scatter(
                full_bias.astype(jnp.bfloat16), "mp", scatter_dimension=0, tiled=True
            ).astype(jnp.float32),
        )
        grad_normed = inner_cols(grad_pre, mat_one).reshape(row_count, seq_count, feat_count)
        grad_normed = grad_normed + grad_total
        _, pull_in = jax.vjp(layer_norm, summed, vector_set[0], vector_set[1])
        grad_summed, gain_one, shift_one = pull_in(grad_normed)
        mix_grad = grad_summed.astype(jnp.bfloat16).reshape(-1, feat_count)
        grad_cos = (factor_mix * matmul(mix_grad, cos_feat)).astype(jnp.bfloat16)
        grad_sin = (-factor_mix * matmul(mix_grad, sin_feat)).astype(jnp.bfloat16)
        cos_rows = grad_cos.reshape(row_count, seq_count, feat_count)
        sin_rows = grad_sin.reshape(row_count, seq_count, feat_count)
        pieces = (
            lax.all_gather(cos_rows, "mp", axis=0, tiled=True),
            lax.all_gather(sin_rows, "mp", axis=0, tiled=True),
        )
        fold_count = pieces[0].shape[0]
        fold_cosine, fold_sine = angles(own_rows, jnp.arange(fold_count, dtype=jnp.int32), L)
        grad_mix = (
            matmul(fold_cosine, pieces[0].reshape(fold_count, -1))
            + matmul(fold_sine, pieces[1].reshape(fold_count, -1))
        ).reshape(row_count, seq_count, feat_count)
        grad = grad_summed + grad_mix
        layer_grads[layer_at] = (
            grad_one,
            grad_two,
            grad_bias_one,
            jnp.stack([gain_one, shift_one, grad_bias_two, gain_two, shift_two]),
        )
    stack_in = jnp.stack([entry[0] for entry in layer_grads])
    stack_out = jnp.stack([entry[1] for entry in layer_grads])
    stack_bias = jnp.stack([entry[2] for entry in layer_grads])
    stack_vec = jnp.stack([entry[3] for entry in layer_grads])
    sum_in, sum_out, sum_bias, sum_vec = (
        lax.psum(stack_in.astype(jnp.bfloat16), "dp").astype(jnp.float32),
        lax.psum(stack_out.astype(jnp.bfloat16), "dp").astype(jnp.float32),
        lax.psum(stack_bias.astype(jnp.bfloat16), "dp").astype(jnp.float32),
        lax.psum(stack_vec.astype(jnp.bfloat16), "dp").astype(jnp.float32),
    )
    local_squares = (
        jnp.sum(sum_in * sum_in) + jnp.sum(sum_out * sum_out) + jnp.sum(sum_bias * sum_bias)
    )
    sum_vec, total_squares = lax.psum((sum_vec, local_squares), "mp")
    grad_norm = jnp.sqrt(total_squares + jnp.sum(sum_vec * sum_vec))
    factor = jnp.minimum(1.0, CLIP / grad_norm)
    m_in, v_in, w_in = adamw(
        weight_in, sum_in * factor, moment_in, square_in, 1.0 / math.sqrt(D), DECAY
    )
    m_out, v_out, w_out = adamw(
        weight_out, sum_out * factor, moment_out, square_out, 1.0 / math.sqrt(FF), DECAY
    )
    m_bias, v_bias, b_new = adamw(bias_in, sum_bias * factor, moment_bias, square_bias, 0.5, 0.0)
    m_vec, v_vec, vec_new = adamw(vectors, sum_vec * factor, moment_vec, square_vec, 0.5, 0.0)
    return (
        activations,
        grad,
        grad_norm,
        m_in,
        v_in,
        w_in,
        w_in.astype(jnp.bfloat16),
        m_out,
        v_out,
        w_out,
        w_out.astype(jnp.bfloat16),
        m_bias,
        v_bias,
        b_new,
        m_vec,
        v_vec,
        vec_new,
    )


def solution(mesh):
    return jax.shard_map(
        on_device,
        mesh=mesh,
        in_specs=(
            P("mp", "dp", None),
            P("mp", "dp", None),
            P(None, None, "mp"),
            P(None, "mp"),
            P(None, "mp", None),
            P(),
            P(None, None, "mp"),
            P(None, None, "mp"),
            P(None, "mp"),
            P(None, "mp"),
            P(None, "mp", None),
            P(None, "mp", None),
            P(),
            P(),
        ),
        out_specs=(
            P("mp", "dp", None),
            P("mp", "dp", None),
            P(),
            P(None, None, "mp"),
            P(None, None, "mp"),
            P(None, None, "mp"),
            P(None, None, "mp"),
            P(None, "mp", None),
            P(None, "mp", None),
            P(None, "mp", None),
            P(None, "mp", None),
            P(None, "mp"),
            P(None, "mp"),
            P(None, "mp"),
            P(),
            P(),
            P(),
        ),
        check_vma=False,
    )
```

profile of v0, /device:TPU:0, one launch (start us, length us, event | category | flops | bytes accessed | tf_op | source)
XLA Modules:
  0.0 1053.4 jit_solution(13324762968967438915)
XLA Ops:
  13.1 64.2 %all-reduce.6 = (bf16[3072]{0:T(1024)(128)(2,1)S(1)}, bf16[3072]{0:T(1024)(128)(2,1)S(1)}) all-reduce(bf16[3072]{0:T(1024)(128)(2,1)S(1)} %dynamic-update-slice.1, bf16[3072]{0:T(1024)(128)(2,1)S(1)} %dynamic-update-slice), channel_id=6, replica_groups=mesh['dp'=2,'mp'=16] {'mp'}, use_global_device_ids=true, to_apply=%add.1 | all-reduce | flops 6144 | bytes 24576
  77.4 19.5 %fusion.109.clone.2 = bf16[256,768]{1,0:T(8,128)(2,1)S(1)} fusion(bf16[4096,1,768]{2,0,1:T(8,128)(2,1)} %all-gather.21.cloned.1.call-done, s32[256]{0:T(256)S(1)} %iota_add_fusion), kind=kOutput, calls=%fused_computation.114.clone.clone.clone | convolution fusion | flops 1626537984 | bytes 6685696 | tf_op jit(solution)/shard_map/dot_general | solution.py:30
  106.6 17.3 %fusion.112.clone.1.clone.5 = bf16[256,768]{1,0:T(8,128)(2,1)S(1)} fusion(bf16[4096,1,768]{2,0,1:T(8,128)(2,1)S(1)} %copy-done.55, s32[256]{0:T(256)S(1)} %iota_add_fusion), kind=kOutput, calls=%fused_computation.115.clone.clone.clone.clone.clone.2 | convolution fusion | flops 1626537984 | bytes 6685696 | tf_op jit(solution)/shard_map/dot_general | solution.py:30
  123.9 10.9 %fusion.250 = (f32[256]{0:T(256)S(1)}, f32[256,1,768]{2,0,1:T(8,128)S(1)}) fusion(f32[256,768]{1,0:T(8,128)S(1)} %fusion.126, bf16[256,1,768]{2,0,1:T(8,128)(2,1)S(1)} %copy-done.12, bf16[256,768]{1,0:T(8,128)(2,1)S(1)} %fusion.112.clone.1.clone.5), kind=kOutput, calls=%fused_computation.282 | convolution fusion | flops 308870912 | bytes 2360320 | tf_op jit(solution)/shard_map/dot_general | solution.py:30
  140.6 45.6 %all-gather.27.cloned.1.call-done = bf16[1,3072,768]{2,1,0:T(8,128)(2,1)} async-done(((bf16[1,192,768]{2,1,0:T(8,128)(2,1)}), bf16[1,3072,768]{2,1,0:T(8,128)(2,1)}) %all-gather.27.cloned.1.call-update) | async-done | bytes 4718608 | tf_op jit(solution)/shard_map/all_gather | solution.py:106
  194.2 59.1 %all-gather.23.cloned.1.call-done = bf16[4096,1,768]{2,0,1:T(8,128)(2,1)} async-done(((bf16[256,1,768]{2,0,1:T(8,128)(2,1)}), bf16[4096,1,768]{2,0,1:T(8,128)(2,1)}) %all-gather.23.cloned.1.call-update) | async-done | bytes 6291472 | tf_op jit(solution)/shard_map/all_gather | solution.py:87
  253.3 19.6 %fusion.115.clone.5 = bf16[256,768]{1,0:T(8,128)(2,1)S(1)} fusion(bf16[4096,1,768]{2,0,1:T(8,128)(2,1)} %all-gather.23.cloned.1.call-done, s32[256]{0:T(256)S(1)} %iota_add_fusion), kind=kOutput, calls=%fused_computation.116.clone.clone.clone.2 | convolution fusion | flops 1626537984 | bytes 6685696 | tf_op jit(solution)/shard_map/dot_general | solution.py:30
  282.5 17.6 %fusion.118.clone.1.clone.5 = bf16[256,768]{1,0:T(8,128)(2,1)S(1)} fusion(bf16[4096,1,768]{2,0,1:T(8,128)(2,1)S(1)} %copy-done.56, s32[256]{0:T(256)S(1)} %iota_add_fusion), kind=kOutput, calls=%fused_computation.117.clone.clone.clone.clone.clone.2 | convolution fusion | flops 1626537984 | bytes 6685696 | tf_op jit(solution)/shard_map/dot_general | solution.py:30
  315.3 48.6 %all-gather.31.cloned.1.call-done = bf16[1,3072,768]{2,1,0:T(8,128)(2,1)} async-done(((bf16[1,192,768]{2,1,0:T(8,128)(2,1)}), bf16[1,3072,768]{2,1,0:T(8,128)(2,1)}) %all-gather.31.cloned.1.call-update) | async-done | bytes 4718608 | tf_op jit(solution)/shard_map/all_gather | solution.py:106
  390.7 10.7 %fusion.106 = bf16[256,768]{1,0:T(8,128)(2,1)} fusion(f32[256,1,768]{2,0,1:T(8,128)S(1)} %get-tuple-element.124, f32[256]{0:T(256)} %copy-done.53), kind=kOutput, calls=%fused_computation.111 | convolution fusion | flops 308674560 | bytes 1180672 | tf_op jit(solution)/shard_map/dot_general | solution.py:30
  406.9 45.4 %all-gather.33.cloned.1.call-done = bf16[4096,768]{1,0:T(8,128)(2,1)} async-done(((bf16[256,768]{1,0:T(8,128)(2,1)}), bf16[4096,768]{1,0:T(8,128)(2,1)}) %all-gather.33.cloned.1.call-update) | async-done | bytes 6291472 | tf_op jit(solution)/shard_map/all_gather | solution.py:156
  452.3 20.6 %fusion.60 = f32[256,768]{1,0:T(8,128)} fusion(bf16[4096,768]{1,0:T(8,128)(2,1)} %all-gather.33.cloned.1.call-done, s32[256]{0:T(256)S(1)} %copy-done.58), kind=kOutput, calls=%fused_computation.71 | convolution fusion | flops 1626341376 | bytes 7078912 | tf_op jit(solution)/shard_map/dot_general | solution.py:30
  472.9 42.7 %all-gather.35.cloned.1.call-done = bf16[4096,768]{1,0:T(8,128)(2,1)} async-done(((bf16[256,768]{1,0:T(8,128)(2,1)}), bf16[4096,768]{1,0:T(8,128)(2,1)}) %all-gather.35.cloned.1.call-update) | async-done | bytes 6291472 | tf_op jit(solution)/shard_map/all_gather | solution.py:157
  515.7 20.6 %multiply_reduce_fusion.1 = (bf16[768]{0:T(1024)(128)(2,1)}, f32[256]{0:T(256)S(1)}, bf16[768]{0:T(1024)(128)(2,1)}, f32[256,1,768]{2,0,1:T(8,128)S(1)}) fusion(f32[256,1,768]{2,0,1:T(8,128)S(1)} %get-tuple-element.137, f32[256]{0:T(256)S(1)} %copy-done.30, f32[256]{0:T(256)S(1)} %copy-done.27, f32[768]{0:T(1024)S(1)} %copy-done.18, ...), kind=kOutput, calls=%fused_computation.137 | convolution fusion | flops 1628502272 | bytes 9448448 | tf_op jit(solution)/shard_map/dot_general | solution.py:30
  563.0 30.6 %reduce-scatter.7.cloned.1.call-done = bf16[768,192]{0,1:T(8,128)(2,1)} async-done(((bf16[768,3072]{0,1:T(8,128)(2,1)}), bf16[768,192]{0,1:T(8,128)(2,1)}) %reduce-scatter.7.cloned.1.call-update) | async-done | bytes 294928 | tf_op jit(solution)/shard_map/reduce_scatter | solution.py:136
  593.6 78.8 %reduce-scatter.5.cloned.1.call-done = bf16[768,192]{0,1:T(8,128)(2,1)} async-done(((bf16[768,3072]{0,1:T(8,128)(2,1)}), bf16[768,192]{0,1:T(8,128)(2,1)}) %reduce-scatter.5.cloned.1.call-update) | async-done | bytes 294928 | tf_op jit(solution)/shard_map/reduce_scatter | solution.py:136
  674.4 76.6 %reduce-scatter.11.cloned.1.call-done = bf16[192,768]{1,0:T(8,128)(2,1)} async-done(((bf16[3072,768]{1,0:T(8,128)(2,1)}), bf16[192,768]{1,0:T(8,128)(2,1)}) %reduce-scatter.11.cloned.1.call-update) | async-done | bytes 294928 | tf_op jit(solution)/shard_map/reduce_scatter | solution.py:139
  750.9 78.8 %reduce-scatter.9.cloned.1.call-done = bf16[192,768]{1,0:T(8,128)(2,1)} async-done(((bf16[3072,768]{1,0:T(8,128)(2,1)}), bf16[192,768]{1,0:T(8,128)(2,1)}) %reduce-scatter.9.cloned.1.call-update) | async-done | bytes 294928 | tf_op jit(solution)/shard_map/reduce_scatter | solution.py:139
  837.5 10.0 fusion.107
  848.0 10.1 fusion.108
  859.2 59.1 %all-reduce.5 = (bf16[3072]{0:T(1024)(128)(2,1)S(1)}, bf16[3072]{0:T(1024)(128)(2,1)S(1)}) all-reduce(bf16[3072]{0:T(1024)(128)(2,1)S(1)} %copy-done.40, bf16[3072]{0:T(1024)(128)(2,1)S(1)} %copy-done.41), channel_id=17, replica_groups=mesh['dp'=2,'mp'=16] {'mp'}, use_global_device_ids=true, to_apply=%region_27.28.clone | all-reduce | flops 6144 | bytes 24576
  933.3 59.1 %all-reduce.4 = (f32[]{:T(128)}, f32[2,5,768]{2,1,0:T(8,128)S(1)}) all-reduce(f32[]{:T(128)S(6)} %add.352, bf16[2,5,768]{2,1,0:T(8,128)(2,1)S(1)} %get-tuple-element.97), channel_id=1, replica_groups=mesh['dp'=2,'mp'=16] {'mp'}, use_global_device_ids=true, to_apply=%region_30.31 | all-reduce | flops 7681 | bytes 46088 | tf_op jit(solution)/shard_map/psum | solution.py:185
  1004.2 19.9 %fusion.59 = f32[256,768]{1,0:T(8,128)S(1)} fusion(bf16[4096,768]{1,0:T(8,128)(2,1)} %all-gather.37.cloned.1.call-done, s32[256]{0:T(256)S(1)} %copy-done.59), kind=kOutput, calls=%fused_computation.70 | convolution fusion | flops 1626341376 | bytes 7078912 | tf_op jit(solution)/shard_map/dot_general | solution.py:30
  1024.1 19.7 %fusion.84 = f32[256,1,768]{2,0,1:T(8,128)S(1)} fusion(f32[256,768]{1,0:T(8,128)S(1)} %fusion.59, bf16[4096,768]{1,0:T(8,128)(2,1)} %all-gather.39.cloned.1.call-done, s32[256]{0:T(256)S(1)} %copy-done.59, f32[256,1,768]{2,0,1:T(8,128)S(1)} %copy-done.11, f32[256]{0:T(256)S(1)} %copy-done.52), kind=kOutput, calls=%fused_computation.101 | convolution fusion | flops 1626931200 | bytes 8652800 | tf_op jit(solution)/shard_map/dot_general | solution.py:30
  (263 shorter events, 147.3 us)
Async XLA Ops:
  7.2 70.2 %all-gather.21.cloned.1.call-start = ((), (), s32[]{:S(2)}) async-start(), calls=%async_computation.4 | async-start | bytes 6684672 | tf_op jit(solution)/shard_map/all_gather | solution.py:87
  8.0 127.1 %all-gather.25.cloned.1.call-start = ((), (), s32[]{:S(2)}) async-start(), calls=%async_computation.10 | async-start | bytes 5013504 | tf_op jit(solution)/shard_map/all_gather | solution.py:105
  10.2 176.0 %all-gather.27.cloned.1.call-start = ((), (), s32[]{:S(2)}) async-start(), calls=%async_computation.11 | async-start | bytes 5013504 | tf_op jit(solution)/shard_map/all_gather | solution.py:106
  11.2 242.1 %all-gather.23.cloned.1.call-start = ((), (), s32[]{:S(2)}) async-start(), calls=%async_computation.5 | async-start | bytes 6684672 | tf_op jit(solution)/shard_map/all_gather | solution.py:87
  77.3 205.2 %copy-start.57 = (s32[256]{0:T(256)}, s32[256]{0:T(256)S(1)}, u32[]{:S(2)}) copy-start(s32[256]{0:T(256)S(1)} %iota_add_fusion) | copy-start | bytes 3076
  77.4 222.7 %copy-start.17 = (f32[768]{0:T(1024)}, f32[768]{0:T(1024)S(1)}, u32[]{:S(2)}) copy-start(f32[768]{0:T(1024)S(1)} %get-tuple-element.84) | copy-start | bytes 9220
  192.8 117.1 %all-gather.29.cloned.1.call-start = ((), (), s32[]{:S(2)}) async-start(), calls=%async_computation.12 | async-start | bytes 5013504 | tf_op jit(solution)/shard_map/all_gather | solution.py:105
  193.4 170.5 %all-gather.31.cloned.1.call-start = ((), (), s32[]{:S(2)}) async-start(), calls=%async_computation.13 | async-start | bytes 5013504 | tf_op jit(solution)/shard_map/all_gather | solution.py:106
  193.9 258.4 %all-gather.33.cloned.1.call-start = ((), (), s32[]{:S(2)}) async-start(), calls=%async_computation.14 | async-start | bytes 6684672 | tf_op jit(solution)/shard_map/all_gather | solution.py:156
  390.4 125.2 %all-gather.35.cloned.1.call-start = ((), (), s32[]{:S(2)}) async-start(), calls=%async_computation.15 | async-start | bytes 6684672 | tf_op jit(solution)/shard_map/all_gather | solution.py:157
  401.3 192.3 %reduce-scatter.7.cloned.1.call-start = ((), (), s32[]{:S(2)}) async-start(), calls=%async_computation.7 | async-start | bytes 5013504 | tf_op jit(solution)/shard_map/reduce_scatter | solution.py:136
  406.6 265.8 %reduce-scatter.5.cloned.1.call-start = ((), (), s32[]{:S(2)}) async-start(), calls=%async_computation.6 | async-start | bytes 5013504 | tf_op jit(solution)/shard_map/reduce_scatter | solution.py:136
  549.3 201.6 %reduce-scatter.11.cloned.1.call-start = ((), (), s32[]{:S(2)}) async-start(), calls=%async_computation.9 | async-start | bytes 5013504 | tf_op jit(solution)/shard_map/reduce_scatter | solution.py:139
  556.6 273.1 %reduce-scatter.9.cloned.1.call-start = ((), (), s32[]{:S(2)}) async-start(), calls=%async_computation.8 | async-start | bytes 5013504 | tf_op jit(solution)/shard_map/reduce_scatter | solution.py:139
  563.0 364.3 %all-reduce.11.cloned.1.call-start = ((), (), s32[]{:S(2)}) async-start(), calls=%async_computation.18 | async-start | bytes 2359296 | tf_op jit(solution)/shard_map/psum | solution.py:177
  831.7 172.5 %all-gather.37.cloned.1.call-start = ((), (), s32[]{:S(2)}) async-start(), calls=%async_computation.16 | async-start | bytes 6684672 | tf_op jit(solution)/shard_map/all_gather | solution.py:156
  847.7 146.8 %copy-start.16 = (f32[2,5,768]{2,0,1:T(2,128)S(1)}, f32[2,5,768]{2,0,1:T(2,128)}, u32[]{:S(2)}) copy-start(f32[2,5,768]{2,0,1:T(2,128)} %param.19) | copy-start | bytes 92164
  847.7 146.8 %copy-start.19 = (f32[2,5,768]{2,0,1:T(2,128)S(1)}, f32[2,5,768]{2,0,1:T(2,128)}, u32[]{:S(2)}) copy-start(f32[2,5,768]{2,0,1:T(2,128)} %param.27) | copy-start | bytes 92164
  847.7 146.8 %copy-start.20 = (f32[2,5,768]{2,0,1:T(2,128)S(1)}, f32[2,5,768]{2,0,1:T(2,128)}, u32[]{:S(2)}) copy-start(f32[2,5,768]{2,0,1:T(2,128)} %param.26) | copy-start | bytes 92164
  847.7 148.7 %copy-start.39 = (f32[2,192]{1,0:T(2,128)S(1)}, f32[2,192]{1,0:T(2,128)}, u32[]{:S(2)}) copy-start(f32[2,192]{1,0:T(2,128)} %param.17) | copy-start | bytes 4612
  847.7 148.7 %copy-start.42 = (f32[2,192]{1,0:T(2,128)S(1)}, f32[2,192]{1,0:T(2,128)}, u32[]{:S(2)}) copy-start(f32[2,192]{1,0:T(2,128)} %param.23) | copy-start | bytes 4612
  847.7 148.7 %copy-start.43 = (f32[2,192]{1,0:T(2,128)S(1)}, f32[2,192]{1,0:T(2,128)}, u32[]{:S(2)}) copy-start(f32[2,192]{1,0:T(2,128)} %param.22) | copy-start | bytes 4612
  847.7 176.4 %all-gather.39.cloned.1.call-start = ((), (), s32[]{:S(2)}) async-start(), calls=%async_computation.17 | async-start | bytes 6684672 | tf_op jit(solution)/shard_map/all_gather | solution.py:157
  858.0 139.0 %copy-start.7 = (f32[2,768,192]{1,2,0:T(8,128)S(1)}, f32[2,768,192]{1,2,0:T(8,128)}, u32[]{:S(2)}) copy-start(f32[2,768,192]{1,2,0:T(8,128)} %param.21) | copy-start | bytes 3538948
  (57 other events, 1544.2 us)
Sparse Core Ops, SparseCore 0:
  10.3 65.1 all-gather.20
  78.3 53.0 all-gather.24
  134.3 51.8 all-gather.26
  192.9 60.3 all-gather.22
  256.0 53.1 all-gather.28
  312.0 51.8 all-gather.30
  390.6 61.6 all-gather.32
  455.2 60.4 all-gather.34
  519.5 74.0 reduce-scatter.6
  597.8 74.5 reduce-scatter.4
  676.3 74.5 reduce-scatter.10
  755.1 74.5 reduce-scatter.8
  833.2 42.1 all-reduce.10
  877.8 62.3 all-gather.36
  942.6 60.5 all-gather.38
where the time goes:
time: 1060 us; the launch traced here: 1050 us
  waiting for transfers between devices  508 us (48%)
  matrix products  296 us (28%)
  blocking collectives  191 us (18%)
  other arithmetic  25 us (2%)
  between operations  21.1 us (2%)
  local copies, waits for them, and re-layouts  11.2 us (1%)
    dot_general x20, matrix products, matmul(): return jnp.dot(left_op, right_op, preferred_element_type=jnp.float32)  257 us
    reduce_scatter x2, waiting for transfers between devices, on_device(): lax.psum_scatter(full_two.astype(jnp.bfloat16), 'mp', scatter_dimension=0...  155 us
    unnamed x2, blocking collectives  123 us
    reduce_scatter x2, waiting for transfers between devices, on_device(): lax.psum_scatter(full_one.astype(jnp.bfloat16), 'mp', scatter_dimension=1...  109 us
    all_gather x2, waiting for transfers between devices, on_device(): lax.all_gather(weight_two, 'mp', axis=0, tiled=True)  94.2 us
    all_gather x2, waiting for transfers between devices, on_device(): piece = lax.all_gather(rounded, 'mp', axis=0, tiled=True)  59.2 us
    psum x1, blocking collectives, on_device(): sum_vec, total_squares = lax.psum((sum_vec, local_squares), 'mp')  59.1 us
    all_gather x2, waiting for transfers between devices, on_device(): lax.all_gather(cos_rows, 'mp', axis=0, tiled=True)  45.4 us
  transfers between devices with their start and end apart: 15, of which 9 were waited for; matrix products, arithmetic and copies ran while one was open for 26% of the time, Pallas kernels for 0%

commit v1 on v0

--- a/solution.py
+++ b/solution.py
@@ -1,8 +1,13 @@
+import functools
 import math
 
 import jax
 import jax.numpy as jnp
+import ml_dtypes
+import numpy as np
 from jax import lax
+from jax.experimental import pallas as pl
+from jax.experimental.pallas import tpu as pltpu
 from jax.sharding import PartitionSpec as P
 
 D = 768
@@ -18,12 +23,208 @@
 EPS_ADAM = 1e-08
 EPS_NORM = 1e-05
 DECAY = 0.01
-
-
-def angles(row_ids, col_ids, period):
-    product = row_ids[:, None] * col_ids[None, :] % period
-    angle_grid = product.astype(jnp.float32) * (2.0 * math.pi / period)
-    return (jnp.cos(angle_grid).astype(jnp.bfloat16), jnp.sin(angle_grid).astype(jnp.bfloat16))
+MESH = pl.DeviceIdType.MESH
+F32 = jnp.float32
+BF16 = jnp.bfloat16
+
+
+class Plan:
+    def __init__(self, parts):
+        self.parts = parts
+        self.rows = L // parts
+        self.inner = self.rows // parts
+        self.pairs = D // 2 // parts
+        self.feats = -(-2 * self.pairs // 16) * 16
+        rows, inner = self.rows, self.inner
+        lane = np.arange(rows)
+        self.place = parts * (lane % inner) + lane // inner
+        packed = np.zeros((parts, self.feats, D))
+        rebuild = np.zeros((parts, self.feats, D))
+        n = np.arange(D)
+        for at in range(parts):
+            for i in range(self.pairs):
+                m = self.pairs * at + i
+                a, b = i, self.pairs + i
+                packed[at, a] = np.cos(2 * np.pi * (m * n % D) / D)
+                rebuild[at, a, m] = 1.0
+                if m == 0:
+                    packed[at, b] = np.cos(2 * np.pi * (D // 2 * n % D) / D)
+                    rebuild[at, b, D // 2] = 1.0
+                else:
+                    packed[at, b] = np.sin(2 * np.pi * (m * n % D) / D)
+                    rebuild[at, a, D - m] = 1.0
+                    rebuild[at, b, m] = -1.0
+                    rebuild[at, b, D - m] = 1.0
+        bf = ml_dtypes.bfloat16
+        self.packed = packed.reshape(-1, D).astype(bf)
+        self.rebuild = rebuild.reshape(-1, D).astype(bf)
+        turn = 2 * np.pi * (np.arange(parts)[:, None] * self.place[None, :] % L) / L
+        self.turn = np.stack([np.cos(turn), np.sin(turn)]).astype(np.float32)
+        angle = 2 * np.pi * (self.place[:, None] * np.arange(rows)[None, :] % rows) / rows
+        self.wave = np.concatenate([np.cos(angle), np.sin(angle)]).astype(bf)
+
+
+def half_dft(values):
+    n = len(values)
+    if n == 1:
+        return [(values[0], None)]
+    if n == 2:
+        return [(values[0] + values[1], None), (values[0] - values[1], None)]
+    even, odd = half_dft(values[0::2]), half_dft(values[1::2])
+    half = n // 2
+    result = [None] * (half + 1)
+    for k in range(half // 2 + 1):
+        er, ei = even[k]
+        orr, oi = odd[k]
+        if k == 0:
+            result[0] = (er + orr, None)
+            result[half] = (er - orr, None)
+        elif 2 * k == half:
+            result[k] = (er, -orr)
+        else:
+            c, s = math.cos(2 * math.pi * k / n), math.sin(2 * math.pi * k / n)
+            tr, ti = orr * c + oi * s, oi * c - orr * s
+            result[k] = (er + tr, ei + ti)
+            result[half - k] = (er - tr, ti - ei)
+    return result
+
+
+def position_dft(plan, me, recv, work, send, turn_ref, wave_ref):
+    parts, feats, rows, inner, pairs = plan.parts, plan.feats, plan.rows, plan.inner, plan.pairs
+    chunk = 16
+    lanes = min(rows, 128)
+    for lane_at in range(0, rows, lanes):
+
+        def body(i, carry):
+            at = pl.multiple_of(i * chunk, chunk)
+            values = [recv[p, pl.ds(at, chunk), lane_at : lane_at + lanes].astype(F32) for p in range(parts)]
+            outs = half_dft(values)
+            row = at + lax.broadcasted_iota(jnp.int32, (chunk, lanes), 0)
+            is_sine = (row >= pairs) & jnp.logical_not((row == pairs) & (me == 0))
+            for d in range(parts):
+                re, im = outs[min(d, parts - d)]
+                im = jnp.zeros_like(re) if im is None else im
+                if d > parts - d:
+                    im = -im
+                re, im = jnp.where(is_sine, -im, re), jnp.where(is_sine, re, im)
+                c = turn_ref[0, d : d + 1, lane_at : lane_at + lanes]
+                s = turn_ref[1, d : d + 1, lane_at : lane_at + lanes]
+                work[d, pl.ds(at, chunk), lane_at : lane_at + lanes] = (re * c + im * s).astype(BF16)
+                work[d, pl.ds(at, chunk), rows + lane_at : rows + lane_at + lanes] = (im * c - re * s).astype(BF16)
+            return carry
+
+        lax.fori_loop(0, feats // chunk, body, 0)
+
+    def swap(i, carry):
+        at = pl.multiple_of(i * chunk, chunk)
+        outs = [
+            jnp.dot(work[d, pl.ds(at, chunk), :], wave_ref[...], preferred_element_type=F32)
+            for d in range(parts)
+        ]
+        group = lax.broadcasted_iota(jnp.int32, (chunk, rows), 1) // inner
+        bit = 1
+        while bit < parts:
+            upper = (group // bit) % 2 == 1
+            for d in range(parts):
+                if d & bit:
+                    continue
+                low, high = outs[d], outs[d | bit]
+                shift = inner * bit
+                outs[d] = jnp.where(upper, pltpu.roll(high, shift, 1), low)
+                outs[d | bit] = jnp.where(upper, high, pltpu.roll(low, rows - shift, 1))
+            bit *= 2
+        for q in range(parts):
+            send[q, pl.ds(at, chunk), :] = outs[q].astype(BF16)
+        return carry
+
+    lax.fori_loop(0, feats // chunk, swap, 0)
+
+
+def exchange(plan, me, send, recv, send_sem, recv_sem):
+    parts = plan.parts
+
+    def copy_to(k):
+        q = lax.rem(me + k, parts)
+        return pltpu.make_async_remote_copy(
+            src_ref=send.at[q],
+            dst_ref=recv.at[me],
+            send_sem=send_sem.at[q],
+            recv_sem=recv_sem.at[me],
+            device_id={"mp": q},
+            device_id_type=MESH,
+        )
+
+    def copy_from(k):
+        p = lax.rem(me + k, parts)
+        return pltpu.make_async_remote_copy(
+            src_ref=send.at[p],
+            dst_ref=recv.at[p],
+            send_sem=send_sem.at[p],
+            recv_sem=recv_sem.at[p],
+            device_id={"mp": p},
+            device_id_type=MESH,
+        )
+
+    def start(k, carry):
+        copy_to(k).start()
+        return carry
+
+    def finish(k, carry):
+        copy_from(k).wait_recv()
+        return carry
+
+    def drain(k, carry):
+        copy_to(k).wait_send()
+        return carry
+
+    lax.fori_loop(1, parts, start, 0)
+    recv[me] = send[me]
+    lax.fori_loop(1, parts, finish, 0)
+    lax.fori_loop(1, parts, drain, 0)
+
+
+def mix_kernel(plan, x_ref, packed_ref, rebuild_ref, turn_ref, wave_ref, out_ref, send, recv, work, send_back, recv_back, sems):
+    me = lax.axis_index("mp")
+    parts, feats, rows = plan.parts, plan.feats, plan.rows
+    barrier = pltpu.get_barrier_semaphore()
+
+    def greet(k, carry):
+        pl.semaphore_signal(barrier, inc=1, device_id={"mp": lax.rem(me + k, parts)}, device_id_type=MESH)
+        return carry
+
+    lax.fori_loop(1, parts, greet, 0)
+    pl.semaphore_wait(barrier, parts - 1)
+
+    columns = lax.dot_general(packed_ref[...], x_ref[...], (((1,), (1,)), ((), ())), preferred_element_type=F32)
+    send[...] = columns.astype(BF16).reshape(parts, feats, rows)
+    exchange(plan, me, send, recv, sems.at[0], sems.at[1])
+    position_dft(plan, me, recv, work, send_back, turn_ref, wave_ref)
+    exchange(plan, me, send_back, recv_back, sems.at[2], sems.at[3])
+    mixed = lax.dot_general(
+        recv_back[...].reshape(parts * feats, rows), rebuild_ref[...], (((0,), (0,)), ((), ())), preferred_element_type=F32
+    )
+    out_ref[...] = mixed * (1.0 / math.sqrt(L * D))
+
+
+def mix(plan, value):
+    block = (plan.parts, plan.feats, plan.rows)
+    return pl.pallas_call(
+        functools.partial(mix_kernel, plan),
+        out_shape=jax.ShapeDtypeStruct((plan.rows, D), F32),
+        in_specs=[pl.BlockSpec(memory_space=pltpu.VMEM)] * 5,
+        out_specs=pl.BlockSpec(memory_space=pltpu.VMEM),
+        scratch_shapes=[
+            pltpu.VMEM(block, BF16),
+            pltpu.VMEM(block, BF16),
+            pltpu.VMEM((plan.parts, plan.feats, 2 * plan.rows), BF16),
+            pltpu.VMEM(block, BF16),
+            pltpu.VMEM(block, BF16),
+            pltpu.SemaphoreType.DMA((4, plan.parts)),
+        ],
+        compiler_params=pltpu.CompilerParams(
+            collective_id=0, has_side_effects=True, vmem_limit_bytes=40 * 2**20
+        ),
+    )(value, plan.packed, plan.rebuild, plan.turn, plan.wave)
 
 
 def matmul(left_op, right_op):
@@ -74,27 +275,20 @@
     square_vec,
 ):
     row_count, seq_count, feat_count = tokens.shape
-    offset = lax.axis_index("mp") * row_count
-    own_rows = offset + jnp.arange(row_count, dtype=jnp.int32)
-    feature_ids = jnp.arange(feat_count, dtype=jnp.int32)
-    cos_feat, sin_feat = angles(feature_ids, feature_ids, feat_count)
-    factor_mix = 1.0 / math.sqrt(L * D)
-    current = tokens.astype(jnp.float32)
+    plan = Plan(L // row_count)
+
+    def localize(value):
+        return jnp.swapaxes(value.reshape(plan.inner, plan.parts, -1), 0, 1).reshape(value.shape)
+
+    def restore(value):
+        return jnp.swapaxes(value.reshape(plan.parts, plan.inner, -1), 0, 1).reshape(value.shape)
+
+    current = localize(tokens).astype(jnp.float32)
     saved = []
     for layer_at in range(LAYERS):
         vector_set = vectors[layer_at]
         rounded = current.astype(jnp.bfloat16)
-        piece = lax.all_gather(rounded, "mp", axis=0, tiled=True)
-        count = piece.shape[0]
-        cosine, sine = angles(own_rows, jnp.arange(count, dtype=jnp.int32), L)
-        flat = piece.reshape(count, -1)
-        spec_cos = matmul(cosine, flat)
-        spec_sin = matmul(sine, flat)
-        spec_cos = spec_cos.astype(jnp.bfloat16)
-        spec_sin = spec_sin.astype(jnp.bfloat16)
-        mixed = (factor_mix * (matmul(spec_cos, cos_feat) - matmul(spec_sin, sin_feat))).reshape(
-            row_count, seq_count, feat_count
-        )
+        mixed = mix(plan, rounded.reshape(row_count, feat_count)).reshape(row_count, seq_count, feat_count)
         summed = current + mixed
         normed = layer_norm(summed, vector_set[0], vector_set[1])
         hidden_in = normed.astype(jnp.bfloat16)
@@ -114,8 +308,8 @@
         total = normed + branch + vector_set[2]
         current = layer_norm(total, vector_set[3], vector_set[4])
         saved.append((summed, total, pre_act, acts, held))
-    activations = current.astype(jnp.bfloat16)
-    grad = cotangent.astype(jnp.float32)
+    activations = restore(current.astype(jnp.bfloat16))
+    grad = localize(cotangent).astype(jnp.float32)
     layer_grads = [None] * LAYERS
     for layer_at in reversed(range(LAYERS)):
         vector_set = vectors[layer_at]
@@ -148,20 +342,7 @@
         _, pull_in = jax.vjp(layer_norm, summed, vector_set[0], vector_set[1])
         grad_summed, gain_one, shift_one = pull_in(grad_normed)
         mix_grad = grad_summed.astype(jnp.bfloat16).reshape(-1, feat_count)
-        grad_cos = (factor_mix * matmul(mix_grad, cos_feat)).astype(jnp.bfloat16)
-        grad_sin = (-factor_mix * matmul(mix_grad, sin_feat)).astype(jnp.bfloat16)
-        cos_rows = grad_cos.reshape(row_count, seq_count, feat_count)
-        sin_rows = grad_sin.reshape(row_count, seq_count, feat_count)
-        pieces = (
-            lax.all_gather(cos_rows, "mp", axis=0, tiled=True),
-            lax.all_gather(sin_rows, "mp", axis=0, tiled=True),
-        )
-        fold_count = pieces[0].shape[0]
-        fold_cosine, fold_sine = angles(own_rows, jnp.arange(fold_count, dtype=jnp.int32), L)
-        grad_mix = (
-            matmul(fold_cosine, pieces[0].reshape(fold_count, -1))
-            + matmul(fold_sine, pieces[1].reshape(fold_count, -1))
-        ).reshape(row_count, seq_count, feat_count)
+        grad_mix = mix(plan, mix_grad).reshape(row_count, seq_count, feat_count)
         grad = grad_summed + grad_mix
         layer_grads[layer_at] = (
             grad_one,
@@ -195,7 +376,7 @@
     m_vec, v_vec, vec_new = adamw(vectors, sum_vec * factor, moment_vec, square_vec, 0.5, 0.0)
     return (
         activations,
-        grad,
+        restore(grad),
         grad_norm,
         m_in,
         v_in,

time: 1060 us -> 780 us (0.74)
  matrix products: 296 us -> 60 us
  waiting for transfers between devices: 508 us -> 343 us
  Pallas kernels: 0 us -> 107 us
    dot_general x20 -> x4, matrix products: 257 us -> 22.4 us  [matmul(): return jnp.dot(left_op, right_op, preferred_element_type=jnp.float32)]
    all_gather x6 -> x0, waiting for transfers between devices: 147 us -> none  [the longest x2 59.2 us: on_device(): piece = lax.all_gather(rounded, 'mp', axis=0, tiled=True)]
    pallas_call x0 -> x4, Pallas kernels: none -> 107 us  [mix(): pl.pallas_call(functools.partial(mix_kernel, plan), out_shape=jax.ShapeDt...]
    all_gather x2, waiting for transfers between devices: 94.2 us -> 64.6 us  [on_device(): lax.all_gather(weight_two, 'mp', axis=0, tiled=True)]
    all_gather x2, waiting for transfers between devices: 0.04 us -> 27.2 us  [on_device(): lax.all_gather(weight_one, 'mp', axis=1, tiled=True)]
    reduce_scatter x2, waiting for transfers between devices: 109 us -> 94.1 us  [on_device(): lax.psum_scatter(full_one.astype(jnp.bfloat16), 'mp', scatter_dimension=1...]
  transfers between devices with their start and end apart: 15 -> 9, of which waited for: 9 -> 7; matrix products, arithmetic and copies ran while one was open for 26% -> 8% of each run, Pallas kernels for 0% -> 14%
where the time goes in v1:
time: 780 us; the launch traced here: 770 us
  waiting for transfers between devices  343 us (44%)
  blocking collectives  195 us (25%)
  Pallas kernels  107 us (14%)
  matrix products  60 us (8%)
  other arithmetic  27.5 us (4%)
  between operations  20.7 us (3%)
  local copies, waits for them, and re-layouts  16 us (2%)
    reduce_scatter x2, waiting for transfers between devices, on_device(): lax.psum_scatter(full_two.astype(jnp.bfloat16), 'mp', scatter_dimension=0...  156 us
    unnamed x2, blocking collectives  128 us
    pallas_call x4, Pallas kernels, mix(): pl.pallas_call(functools.partial(mix_kernel, plan), out_shape=jax.ShapeDt...  107 us
    reduce_scatter x2, waiting for transfers between devices, on_device(): lax.psum_scatter(full_one.astype(jnp.bfloat16), 'mp', scatter_dimension=1...  94.1 us
    all_gather x2, waiting for transfers between devices, on_device(): lax.all_gather(weight_two, 'mp', axis=0, tiled=True)  64.6 us
    psum x1, blocking collectives, on_device(): sum_vec, total_squares = lax.psum((sum_vec, local_squares), 'mp')  58 us
    all_gather x2, waiting for transfers between devices, on_device(): lax.all_gather(weight_one, 'mp', axis=1, tiled=True)  27.2 us
    dot_general x4, matrix products, matmul(): return jnp.dot(left_op, right_op, preferred_element_type=jnp.float32)  22.4 us
  transfers between devices with their start and end apart: 9, of which 7 were waited for; matrix products, arithmetic and copies ran while one was open for 8% of the time, Pallas kernels for 14%

profile of v1, /device:TPU:0, one launch (start us, length us, event | category | flops | bytes accessed | tf_op | source)
XLA Modules:
  0.0 769.5 jit_solution(13283388106669602550)
XLA Ops:
  16.1 63.9 %all-reduce.6 = (bf16[3072]{0:T(1024)(128)(2,1)S(1)}, bf16[3072]{0:T(1024)(128)(2,1)S(1)}) all-reduce(bf16[3072]{0:T(1024)(128)(2,1)S(1)} %dynamic-update-slice.1, bf16[3072]{0:T(1024)(128)(2,1)S(1)} %dynamic-update-slice), channel_id=6, replica_groups=mesh['dp'=2,'mp'=16] {'mp'}, use_global_device_ids=true, to_apply=%add.1 | all-reduce | flops 6144 | bytes 24576
  80.2 29.6 %shard_map.305 = f32[256,768]{1,0:T(8,128)S(1)} custom-call(bf16[256,768]{1,0:T(8,128)(2,1)S(1)} %bitcast.95, bf16[768,768]{1,0:T(8,128)(2,1)S(1)} %copy-done, bf16[768,768]{1,0:T(8,128)(2,1)S(1)} %copy-done.1, f32[2,16,256]{2,1,0:T(8,128)S(1)} %copy-done.3, bf16[512,256]{1,0:T(8,128)(2,1)S(1)} %copy-done.2), custom_call_target="tpu_custom_call" | custom-call | tf_op jit(solution)/shard_map/pallas_call | solution.py:211
  110.9 5.5 fusion.16
  116.4 15.8 %all-gather.13.cloned.1.call-done = bf16[1,3072,768]{2,1,0:T(8,128)(2,1)} async-done(((bf16[1,192,768]{2,1,0:T(8,128)(2,1)}), bf16[1,3072,768]{2,1,0:T(8,128)(2,1)}) %all-gather.13.cloned.1.call-update) | async-done | bytes 4718608 | tf_op jit(solution)/shard_map/all_gather | solution.py:300
  132.2 5.5 fusion.98
  138.1 30.9 %shard_map.306 = f32[256,768]{1,0:T(8,128)S(1)} custom-call(bf16[256,768]{1,0:T(8,128)(2,1)S(1)} %fusion.65.x_ref, bf16[768,768]{1,0:T(8,128)(2,1)S(1)} %copy-done, bf16[768,768]{1,0:T(8,128)(2,1)S(1)} %copy-done.1, f32[2,16,256]{2,1,0:T(8,128)S(1)} %copy-done.3, bf16[512,256]{1,0:T(8,128)(2,1)S(1)} %copy-done.2), custom_call_target="tpu_custom_call" | custom-call | tf_op jit(solution)/shard_map/pallas_call | solution.py:211
  170.5 27.1 %all-gather.15.cloned.1.call-done = bf16[1,768,3072]{1,2,0:T(8,128)(2,1)} async-done(((bf16[1,768,192]{1,2,0:T(8,128)(2,1)}), bf16[1,768,3072]{1,2,0:T(8,128)(2,1)}) %all-gather.15.cloned.1.call-update) | async-done | bytes 4718608 | tf_op jit(solution)/shard_map/all_gather | solution.py:299
  197.6 5.7 fusion.19
  203.4 48.8 %all-gather.17.cloned.1.call-done = bf16[1,3072,768]{2,1,0:T(8,128)(2,1)} async-done(((bf16[1,192,768]{2,1,0:T(8,128)(2,1)}), bf16[1,3072,768]{2,1,0:T(8,128)(2,1)}) %all-gather.17.cloned.1.call-update) | async-done | bytes 4718608 | tf_op jit(solution)/shard_map/all_gather | solution.py:300
  252.2 5.6 fusion.99
  268.9 5.5 multiply_reduce_fusion
  274.9 23.2 %shard_map.307 = f32[256,768]{1,0:T(8,128)S(1)} custom-call(bf16[256,768]{1,0:T(8,128)(2,1)S(1)} %add_convert_fusion.3.x_ref, bf16[768,768]{1,0:T(8,128)(2,1)S(1)} %copy-done, bf16[768,768]{1,0:T(8,128)(2,1)S(1)} %copy-done.1, f32[2,16,256]{2,1,0:T(8,128)S(1)} %copy-done.3, bf16[512,256]{1,0:T(8,128)(2,1)S(1)} %copy-done.2), custom_call_target="tpu_custom_call" | custom-call | tf_op jit(solution)/shard_map/pallas_call | solution.py:211
  308.5 6.4 convolution_convert_fusion
  315.1 6.4 convolution_convert_fusion.1
  323.2 5.4 multiply_reduce_fusion.2
  328.7 15.4 %reduce-scatter.7.cloned.1.call-done = bf16[768,192]{0,1:T(8,128)(2,1)} async-done(((bf16[768,3072]{0,1:T(8,128)(2,1)}), bf16[768,192]{0,1:T(8,128)(2,1)}) %reduce-scatter.7.cloned.1.call-update) | async-done | bytes 294928 | tf_op jit(solution)/shard_map/reduce_scatter | solution.py:330
  344.1 78.8 %reduce-scatter.5.cloned.1.call-done = bf16[768,192]{0,1:T(8,128)(2,1)} async-done(((bf16[768,3072]{0,1:T(8,128)(2,1)}), bf16[768,192]{0,1:T(8,128)(2,1)}) %reduce-scatter.5.cloned.1.call-update) | async-done | bytes 294928 | tf_op jit(solution)/shard_map/reduce_scatter | solution.py:330
  424.8 76.5 %reduce-scatter.11.cloned.1.call-done = bf16[192,768]{1,0:T(8,128)(2,1)} async-done(((bf16[3072,768]{1,0:T(8,128)(2,1)}), bf16[192,768]{1,0:T(8,128)(2,1)}) %reduce-scatter.11.cloned.1.call-update) | async-done | bytes 294928 | tf_op jit(solution)/shard_map/reduce_scatter | solution.py:333
  501.3 79.0 %reduce-scatter.9.cloned.1.call-done = bf16[192,768]{1,0:T(8,128)(2,1)} async-done(((bf16[3072,768]{1,0:T(8,128)(2,1)}), bf16[192,768]{1,0:T(8,128)(2,1)}) %reduce-scatter.9.cloned.1.call-update) | async-done | bytes 294928 | tf_op jit(solution)/shard_map/reduce_scatter | solution.py:333
  585.7 23.5 %shard_map.308 = f32[256,768]{1,0:T(8,128)S(1)} custom-call(bf16[256,768]{1,0:T(8,128)(2,1)S(1)} %add_convert_fusion.1.x_ref, bf16[768,768]{1,0:T(8,128)(2,1)S(1)} %copy-done, bf16[768,768]{1,0:T(8,128)(2,1)S(1)} %copy-done.1, f32[2,16,256]{2,1,0:T(8,128)S(1)} %copy-done.3, bf16[512,256]{1,0:T(8,128)(2,1)S(1)} %copy-done.2), custom_call_target="tpu_custom_call" | custom-call | tf_op jit(solution)/shard_map/pallas_call | solution.py:211
  611.7 64.5 %all-reduce.5 = (bf16[3072]{0:T(1024)(128)(2,1)S(1)}, bf16[3072]{0:T(1024)(128)(2,1)S(1)}) all-reduce(bf16[3072]{0:T(1024)(128)(2,1)S(1)} %get-tuple-element.128, bf16[3072]{0:T(1024)(128)(2,1)S(1)} %get-tuple-element.130), channel_id=13, replica_groups=mesh['dp'=2,'mp'=16] {'mp'}, use_global_device_ids=true, to_apply=%region_27.0.clone | all-reduce | flops 6144 | bytes 24576
  676.5 8.4 %all-reduce.7 = (bf16[2,5,768]{2,1,0:T(8,128)(2,1)S(1)}, bf16[2,192]{1,0:T(2,128)(2,1)S(1)}) all-reduce(bf16[2,5,768]{2,1,0:T(8,128)(2,1)S(1)} %pad_maximum_fusion.2, bf16[2,192]{1,0:T(2,128)(2,1)S(1)} %pad_maximum_fusion.3), channel_id=1, replica_groups=mesh['dp'=2,'mp'=16] {'dp'}, use_global_device_ids=true, to_apply=%region_41.0 | all-reduce | flops 8064 | bytes 32256 | tf_op jit(solution)/shard_map/psum | solution.py:361
  691.3 58.0 %all-reduce.4 = (f32[]{:T(128)}, f32[2,5,768]{2,1,0:T(8,128)S(1)}) all-reduce(f32[]{:T(128)S(6)} %add.312, bf16[2,5,768]{2,1,0:T(8,128)(2,1)S(1)} %get-tuple-element.80), channel_id=1, replica_groups=mesh['dp'=2,'mp'=16] {'mp'}, use_global_device_ids=true, to_apply=%region_30.0 | all-reduce | flops 7681 | bytes 46088 | tf_op jit(solution)/shard_map/psum | solution.py:366
  753.3 4.7 fusion.84
  (188 shorter events, 54.6 us)
Async XLA Ops:
  7.2 6.2 copy-start.15
  7.2 103.7 %all-gather.11.cloned.1.call-start = ((), (), s32[]{:S(2)}) async-start(), calls=%async_computation.8 | async-start | bytes 5013504 | tf_op jit(solution)/shard_map/all_gather | solution.py:299
  8.6 71.4 %copy-start.20 = (bf16[256,1,768]{2,0,1:T(8,128)(2,1)S(1)}, bf16[256,1,768]{2,0,1:T(8,128)(2,1)}, u32[]{:S(2)}) copy-start(bf16[256,1,768]{2,0,1:T(8,128)(2,1)} %param.18) | copy-start | bytes 1179652
  9.5 70.7 %copy-start = (bf16[768,768]{1,0:T(8,128)(2,1)S(1)}, bf16[768,768]{1,0:T(8,128)(2,1)}, u32[]{:S(2)}) copy-start(bf16[768,768]{1,0:T(8,128)(2,1)} %constant.80.clone.packed_ref) | copy-start | bytes 3538948
  9.5 70.7 %copy-start.1 = (bf16[768,768]{1,0:T(8,128)(2,1)S(1)}, bf16[768,768]{1,0:T(8,128)(2,1)}, u32[]{:S(2)}) copy-start(bf16[768,768]{1,0:T(8,128)(2,1)} %constant.81.clone.rebuild_ref) | copy-start | bytes 3538948
  9.5 70.7 %copy-start.2 = (bf16[512,256]{1,0:T(8,128)(2,1)S(1)}, bf16[512,256]{1,0:T(8,128)(2,1)}, u32[]{:S(2)}) copy-start(bf16[512,256]{1,0:T(8,128)(2,1)} %constant.83.clone.wave_ref) | copy-start | bytes 786436
  9.5 70.7 %copy-start.3 = (f32[2,16,256]{2,1,0:T(8,128)S(1)}, f32[2,16,256]{2,1,0:T(8,128)}, u32[]{:S(2)}) copy-start(f32[2,16,256]{2,1,0:T(8,128)} %constant.82.clone.turn_ref) | copy-start | bytes 98308
  9.5 122.7 %all-gather.13.cloned.1.call-start = ((), (), s32[]{:S(2)}) async-start(), calls=%async_computation.9 | async-start | bytes 5013504 | tf_op jit(solution)/shard_map/all_gather | solution.py:300
  12.0 185.7 %all-gather.15.cloned.1.call-start = ((), (), s32[]{:S(2)}) async-start(), calls=%async_computation.10 | async-start | bytes 5013504 | tf_op jit(solution)/shard_map/all_gather | solution.py:299
  12.7 97.1 %copy-start.23 = (f32[2,5,768]{2,0,1:T(2,128)S(1)}, f32[2,5,768]{2,0,1:T(2,128)}, u32[]{:S(2)}) copy-start(f32[2,5,768]{2,0,1:T(2,128)} %param.23) | copy-start | bytes 92164
  12.7 239.5 %all-gather.17.cloned.1.call-start = ((), (), s32[]{:S(2)}) async-start(), calls=%async_computation.11 | async-start | bytes 5013504 | tf_op jit(solution)/shard_map/all_gather | solution.py:300
  13.3 330.8 %reduce-scatter.7.cloned.1.call-start = ((), (), s32[]{:S(2)}) async-start(), calls=%async_computation.5 | async-start | bytes 5013504 | tf_op jit(solution)/shard_map/reduce_scatter | solution.py:330
  197.6 54.6 %copy-start.28 = (f32[768]{0:T(1024)S(1)}, f32[768]{0:T(1024)}, u32[]{:S(2)}) copy-start(f32[768]{0:T(1024)} %get-tuple-element.63) | copy-start | bytes 9220
  252.2 8.3 %slice-start.2 = ((s8[4718592]{0:T(1024)(128)(4,1)}), s8[4194304]{0:T(1024)(128)(4,1)S(1)}, s32[]{:S(2)}) async-start(s8[4718592]{0:T(1024)(128)(4,1)} %bitcast.109), calls=%async_computation.15 | async-start | bytes 8388608
  252.2 8.3 %slice-start.3 = ((s8[4718592]{0:T(1024)(128)(4,1)}), s8[524288]{0:T(1024)(128)(4,1)S(1)}, s32[]{:S(2)}) async-start(s8[4718592]{0:T(1024)(128)(4,1)} %bitcast.109), calls=%async_computation.16 | async-start | bytes 1048576
  268.8 154.0 %reduce-scatter.5.cloned.1.call-start = ((), (), s32[]{:S(2)}) async-start(), calls=%async_computation.4 | async-start | bytes 5013504 | tf_op jit(solution)/shard_map/reduce_scatter | solution.py:330
  274.4 25.4 %slice-start = ((s8[4718592]{0:T(1024)(128)(4,1)}), s8[4194304]{0:T(1024)(128)(4,1)S(1)}, s32[]{:S(2)}) async-start(s8[4718592]{0:T(1024)(128)(4,1)} %bitcast.107), calls=%async_computation.13 | async-start | bytes 8388608
  274.8 24.9 %slice-start.1 = ((s8[4718592]{0:T(1024)(128)(4,1)}), s8[524288]{0:T(1024)(128)(4,1)S(1)}, s32[]{:S(2)}) async-start(s8[4718592]{0:T(1024)(128)(4,1)} %bitcast.107), calls=%async_computation.14 | async-start | bytes 1048576
  308.3 193.0 %reduce-scatter.11.cloned.1.call-start = ((), (), s32[]{:S(2)}) async-start(), calls=%async_computation.7 | async-start | bytes 5013504 | tf_op jit(solution)/shard_map/reduce_scatter | solution.py:333
  315.0 265.3 %reduce-scatter.9.cloned.1.call-start = ((), (), s32[]{:S(2)}) async-start(), calls=%async_computation.6 | async-start | bytes 5013504 | tf_op jit(solution)/shard_map/reduce_scatter | solution.py:333
  321.5 364.0 %all-reduce.11.cloned.1.call-start = ((), (), s32[]{:S(2)}) async-start(), calls=%async_computation.12 | async-start | bytes 2359296 | tf_op jit(solution)/shard_map/psum | solution.py:358
  609.2 142.0 %copy-start.24 = (f32[2,5,768]{2,0,1:T(2,128)S(1)}, f32[2,5,768]{2,0,1:T(2,128)}, u32[]{:S(2)}) copy-start(f32[2,5,768]{2,0,1:T(2,128)} %param.31) | copy-start | bytes 92164
  609.3 142.0 %copy-start.25 = (f32[2,5,768]{2,0,1:T(2,128)S(1)}, f32[2,5,768]{2,0,1:T(2,128)}, u32[]{:S(2)}) copy-start(f32[2,5,768]{2,0,1:T(2,128)} %param.30) | copy-start | bytes 92164
  609.4 143.8 %copy-start.10 = (f32[2,768,192]{1,2,0:T(8,128)S(1)}, f32[2,768,192]{1,2,0:T(8,128)}, u32[]{:S(2)}) copy-start(f32[2,768,192]{1,2,0:T(8,128)} %param.20) | copy-start | bytes 3538948
  (24 other events, 84.1 us)
Sparse Core Ops, SparseCore 0:
  10.9 56.5 all-gather.10
  70.3 61.8 all-gather.12
  135.1 62.5 all-gather.14
  200.3 51.8 all-gather.16
  268.9 75.0 reduce-scatter.6
  348.3 74.5 reduce-scatter.4
  426.7 74.5 reduce-scatter.10
  505.7 74.5 reduce-scatter.8
  583.8 42.1 all-reduce.10
